TPU v7x, 32 devices: a whole 2x2x4 slice. The times are simulated.
32 devices in a mesh: fsdp: 4 (over z), context: 2 (over x), tensor: 4 (over y, core).
Axes of the slice: x: 2, y: 2, z: 4, core: 2. Of those that a mesh axis runs over, the one named last changes fastest.
Arguments:
- hidden_in: bfloat16 [6144, 1024], P(('fsdp', 'context')), may hold values from -6 to 6
- out_grad: bfloat16 [6144, 1024], P(('fsdp', 'context')), may hold values from -6 to 6
- doc_lengths: int32 [4, 4], P('fsdp'), may hold values from 1 to 1152, as said below
- attn_gain: float32 [1024], replicated, may hold values from 0.5 to 1.5
- q_gain: float32 [128], replicated, may hold values from 0.6 to 1.6
- k_gain: float32 [128], replicated, may hold values from 0.6 to 1.6
- w_query: bfloat16 [1024, 2048], P('fsdp', 'tensor'), may hold values from -0.1875 to 0.1875
- key_projection: bfloat16 [1024, 1024], P('fsdp', 'tensor'), may hold values from -0.1875 to 0.1875
- value_projection: bfloat16 [1024, 1024], P('fsdp', 'tensor'), may hold values from -0.1875 to 0.1875
- w_out: bfloat16 [2048, 1024], P('tensor', 'fsdp'), may hold values from -0.75 to 0.75
- ffn_gain: float32 [1024], replicated, may hold values from 0.5 to 1.5
- w_gate: bfloat16 [1024, 3072], P('fsdp', 'tensor'), may hold values from -0.1875 to 0.1875
- w_up: bfloat16 [1024, 3072], P('fsdp', 'tensor'), may hold values from -0.1875 to 0.1875
- w_down: bfloat16 [3072, 1024], P('tensor', 'fsdp'), may hold values from -0.109375 to 0.109375
Outputs:
- block_out: bfloat16 [6144, 1024], P(('fsdp', 'context'))
- input_grad: float32 [6144, 1024], P(('fsdp', 'context'))
- attn_gain_grad: float32 [1024], replicated
- q_gain_grad: float32 [128], replicated
- k_gain_grad: float32 [128], replicated
- w_query_grad: float32 [1024, 2048], P('fsdp', 'tensor')
- w_key_grad: float32 [1024, 1024], P('fsdp', 'tensor')
- w_value_grad: float32 [1024, 1024], P('fsdp', 'tensor')
- w_out_grad: float32 [2048, 1024], P('tensor', 'fsdp')
- ffn_gain_grad: float32 [1024], replicated
- w_gate_grad: float32 [1024, 3072], P('fsdp', 'tensor')
- w_up_grad: float32 [1024, 3072], P('fsdp', 'tensor')
- w_down_grad: float32 [3072, 1024], P('tensor', 'fsdp')
Inputs may be any that keep to these rules, and one draw needn't show every extreme that they name: `doc_lengths`: each row holds the lengths of 4 documents packed in order into that batch's 1536 places, summing to 1536; one of them, at a position drawn from the seed, has exactly 1152 places, so it starts among the batch's first 768 places and ends among its last 768; the others together take 768 / 2 places.
All inputs are finite; a program needn't handle non-finite values.
Results may differ from a plain program's by a relative error of at most 0.033.
Values may be sent and summed in bfloat16 or wider, within the bound.
A program may use at most 128 MiB of HBM per device.

v0:
```python
import math

import jax
import jax.numpy as jnp
from jax import lax
from jax.sharding import PartitionSpec as P

epsilon = 1e-06
rope_base = 1000000.0
masked_score = -1e30


def inverse_rms(values):
    return lax.rsqrt(jnp.mean(values * values, axis=-1, keepdims=True) + epsilon)


def norm_backward(values, scaling, gain, grads):
    scaled = gain * grads
    cubed = scaling * scaling * scaling
    return scaling * scaled - values * cubed * jnp.mean(scaled * values, axis=-1, keepdims=True)


def doc_layout(lengths_row, positions):
    doc_ends = jnp.cumsum(lengths_row)
    doc_starts = doc_ends - lengths_row
    after_end = positions[:, None] >= doc_ends[None, :]
    inside = (positions[:, None] >= doc_starts[None, :]) & jnp.logical_not(after_end)
    packed_documents = jnp.sum(after_end.astype(jnp.int32), axis=1)
    doc_begin = jnp.sum(jnp.where(inside, doc_starts[None, :], 0), axis=1)
    return (packed_documents, positions - doc_begin)


def rope_tables(positions, head_dim):
    half_dim = head_dim // 2
    freqs = rope_base ** (-(jnp.arange(half_dim, dtype=jnp.float32) * (2.0 / head_dim)))
    angles = positions.astype(jnp.float32)[:, None] * freqs[None, :]
    return (jnp.cos(angles)[:, None, :], jnp.sin(angles)[:, None, :])


def rotate(values, cosine, sine):
    half_dim = values.shape[-1] // 2
    lower, upper = (values[..., :half_dim], values[..., half_dim:])
    return jnp.concatenate([lower * cosine - upper * sine, upper * cosine + lower * sine], axis=-1)


def rotate_back(grads, cosine, sine):
    half_dim = grads.shape[-1] // 2
    lower, upper = (grads[..., :half_dim], grads[..., half_dim:])
    return jnp.concatenate([lower * cosine + upper * sine, upper * cosine - lower * sine], axis=-1)


def on_device(
    hidden_in,
    out_grad,
    doc_lengths,
    attn_gain,
    q_gain,
    k_gain,
    w_query,
    key_projection,
    value_projection,
    w_out,
    ffn_gain,
    w_gate,
    w_up,
    w_down,
):
    tok_rows = hidden_in.shape[0]
    head_dim = q_gain.shape[0]
    q_full, k_full, v_full, o_full = (
        lax.all_gather(w_query, "fsdp", axis=0, tiled=True),
        lax.all_gather(key_projection, "fsdp", axis=0, tiled=True),
        lax.all_gather(value_projection, "fsdp", axis=0, tiled=True),
        lax.all_gather(w_out, "fsdp", axis=1, tiled=True),
    )
    q_heads = q_full.shape[1] // head_dim
    kv_heads = k_full.shape[1] // head_dim
    group_size = q_heads // kv_heads
    inv_sqrt = 1.0 / math.sqrt(head_dim)
    first_row = lax.axis_index("context") * tok_rows
    positions = first_row + jnp.arange(tok_rows, dtype=jnp.int32)
    lengths_row = doc_lengths[0]
    query_docs, query_offsets = doc_layout(lengths_row, positions)
    cosine, sine = rope_tables(query_offsets, head_dim)
    last_query = first_row + tok_rows - 1
    residual_in = hidden_in.astype(jnp.float32)
    scale_one = inverse_rms(residual_in)
    first_normed = (residual_in * scale_one * attn_gain).astype(jnp.bfloat16)
    query_raw = jnp.dot(first_normed, q_full, preferred_element_type=jnp.float32).reshape(
        tok_rows, q_heads, head_dim
    )
    unnormed_key = jnp.dot(first_normed, k_full, preferred_element_type=jnp.float32).reshape(
        tok_rows, kv_heads, head_dim
    )
    values_local = (
        jnp.dot(first_normed, v_full, preferred_element_type=jnp.float32)
        .astype(jnp.bfloat16)
        .reshape(tok_rows, kv_heads, head_dim)
    )
    query_scale = inverse_rms(query_raw)
    key_scale = inverse_rms(unnormed_key)
    query_rows = rotate(query_raw * query_scale * q_gain, cosine, sine).astype(jnp.bfloat16)
    keys_local = rotate(unnormed_key * key_scale * k_gain, cosine, sine).astype(jnp.bfloat16)
    grouped_q = query_rows.reshape(tok_rows, kv_heads, group_size, head_dim)

    def block_mask(key_first, key_count):
        key_places = key_first + jnp.arange(key_count, dtype=jnp.int32)
        key_docs, key_offsets = doc_layout(lengths_row, key_places)
        return (key_places[None, :] <= positions[:, None]) & (
            key_docs[None, :] == query_docs[:, None]
        )

    def attend(running, key_blk, val_blk, key_first):
        best, total, summed = running
        allowed = block_mask(key_first, key_blk.shape[0])
        scores = (
            jnp.einsum("qkgd,skd->kgqs", grouped_q, key_blk, preferred_element_type=jnp.float32)
            * inv_sqrt
        )
        scores = jnp.where(allowed, scores, masked_score)
        new_best = jnp.maximum(best, jnp.max(scores, axis=-1))
        weights = jnp.where(allowed, jnp.exp(scores - new_best[..., None]), 0.0)
        factor = jnp.exp(best - new_best)
        total = total * factor + jnp.sum(weights, axis=-1)
        summed = summed * factor[..., None] + jnp.einsum(
            "kgqs,skd->kgqd",
            weights.astype(jnp.bfloat16),
            val_blk,
            preferred_element_type=jnp.float32,
        )
        return (new_best, total, summed)

    start_state = (
        jnp.full((kv_heads, group_size, tok_rows), masked_score, jnp.float32),
        jnp.zeros((kv_heads, group_size, tok_rows), jnp.float32),
        jnp.zeros((kv_heads, group_size, tok_rows, head_dim), jnp.float32),
    )
    keys_in = lax.all_gather(keys_local, "context", axis=0, tiled=True)
    key_rows = keys_in.shape[0]
    count_of_blocks = key_rows // tok_rows
    key_blocks = keys_in.reshape(count_of_blocks, tok_rows, kv_heads, head_dim)
    val_blocks = lax.all_gather(values_local, "context", axis=0, tiled=True).reshape(
        count_of_blocks, tok_rows, kv_heads, head_dim
    )

    def advance(current, inputs):
        key_blk, val_blk, number = inputs
        block_first = number * tok_rows

        def advance_active(state_in):
            return attend(state_in, key_blk, val_blk, block_first)

        def advance_passed(state_in):
            return state_in

        return (lax.cond(block_first <= last_query, advance_active, advance_passed, current), None)

    result, unused = lax.scan(
        advance, start_state, (key_blocks, val_blocks, jnp.arange(count_of_blocks, dtype=jnp.int32))
    )
    best, total, summed = result
    attn_exact = summed / total[..., None]
    log_total = best + jnp.log(total)
    attention_result = (
        attn_exact.astype(jnp.bfloat16).transpose(2, 0, 1, 3).reshape(tok_rows, q_heads * head_dim)
    )
    attn_out = lax.psum(
        jnp.dot(attention_result, o_full, preferred_element_type=jnp.float32).astype(jnp.bfloat16),
        "tensor",
    ).astype(jnp.float32)
    mixed = residual_in + attn_out
    g_full, u_full, d_full = (
        lax.all_gather(w_gate, "fsdp", axis=0, tiled=True),
        lax.all_gather(w_up, "fsdp", axis=0, tiled=True),
        lax.all_gather(w_down, "fsdp", axis=1, tiled=True),
    )
    scale_two = inverse_rms(mixed)
    normed_two = (mixed * scale_two * ffn_gain).astype(jnp.bfloat16)
    gate = jnp.dot(normed_two, g_full, preferred_element_type=jnp.float32)
    up_part = jnp.dot(normed_two, u_full, preferred_element_type=jnp.float32)
    sigmoid_gate = jax.nn.sigmoid(gate)
    silu_gate = gate * sigmoid_gate
    activated = (silu_gate * up_part).astype(jnp.bfloat16)
    mlp_out = lax.psum(
        jnp.dot(activated, d_full, preferred_element_type=jnp.float32).astype(jnp.bfloat16),
        "tensor",
    ).astype(jnp.float32)
    block_out = (mixed + mlp_out).astype(jnp.bfloat16)
    grad_top = out_grad.astype(jnp.float32)
    down_grad = jnp.einsum("tf,td->fd", activated, out_grad, preferred_element_type=jnp.float32)
    grad_act = jnp.einsum("td,fd->tf", out_grad, d_full, preferred_element_type=jnp.float32)
    silu_slope = sigmoid_gate * (1.0 + gate * (1.0 - sigmoid_gate))
    grad_gate = (grad_act * up_part * silu_slope).astype(jnp.bfloat16)
    grad_up = (grad_act * silu_gate).astype(jnp.bfloat16)
    gate_grad = jnp.einsum("td,tf->df", normed_two, grad_gate, preferred_element_type=jnp.float32)
    up_grad = jnp.einsum("td,tf->df", normed_two, grad_up, preferred_element_type=jnp.float32)
    grad_normed_two = jnp.einsum("tf,df->td", grad_gate, g_full, preferred_element_type=jnp.float32)
    grad_normed_two = grad_normed_two + jnp.einsum(
        "tf,df->td", grad_up, u_full, preferred_element_type=jnp.float32
    )
    grad_normed_two = lax.psum(grad_normed_two.astype(jnp.bfloat16), "tensor").astype(jnp.float32)
    ffn_gain_part = jnp.sum(grad_normed_two * mixed * scale_two, axis=0)
    grad_mixed = grad_top + norm_backward(mixed, scale_two, ffn_gain, grad_normed_two)
    grad_mixed_low = grad_mixed.astype(jnp.bfloat16)
    out_proj_grad = jnp.einsum(
        "th,td->hd", attention_result, grad_mixed_low, preferred_element_type=jnp.float32
    )
    grad_heads = jnp.einsum(
        "td,hd->th", grad_mixed_low, o_full, preferred_element_type=jnp.float32
    ).astype(jnp.bfloat16)
    grad_rows = grad_heads.reshape(tok_rows, kv_heads, group_size, head_dim)
    grad_heads = grad_rows.transpose(1, 2, 0, 3)
    delta = jnp.sum(grad_heads.astype(jnp.float32) * attn_exact, axis=-1)
    back_keys, back_values = (
        lax.all_gather(keys_local, "context", axis=0, tiled=True),
        lax.all_gather(values_local, "context", axis=0, tiled=True),
    )
    key_total = back_keys.shape[0]
    back_count = key_total // tok_rows
    kv_zeros = jnp.zeros((tok_rows, kv_heads, head_dim), jnp.float32)
    dq_zeros = jnp.zeros((tok_rows, kv_heads, group_size, head_dim), jnp.float32)
    key_stack = back_keys.reshape(back_count, tok_rows, kv_heads, head_dim)
    value_stack = back_values.reshape(back_count, tok_rows, kv_heads, head_dim)
    block_numbers = jnp.arange(back_count, dtype=jnp.int32)

    def backstep(dq_running, inputs):
        key_blk, val_blk, number = inputs
        key_first = number * tok_rows

        def backstep_active(dq_in):
            allowed = block_mask(key_first, tok_rows)
            scores = (
                jnp.einsum("qkgd,skd->kgqs", grouped_q, key_blk, preferred_element_type=jnp.float32)
                * inv_sqrt
            )
            probs = jnp.where(allowed, jnp.exp(scores - log_total[..., None]), 0.0)
            grad_probs = jnp.einsum(
                "kgqd,skd->kgqs", grad_heads, val_blk, preferred_element_type=jnp.float32
            )
            grad_scores = (probs * (grad_probs - delta[..., None])).astype(jnp.bfloat16)
            dq_out = (
                dq_in
                + jnp.einsum(
                    "kgqs,skd->qkgd", grad_scores, key_blk, preferred_element_type=jnp.float32
                )
                * inv_sqrt
            )
            key_part = (
                jnp.einsum(
                    "kgqs,qkgd->skd", grad_scores, grouped_q, preferred_element_type=jnp.float32
                )
                * inv_sqrt
            )
            value_part = jnp.einsum(
                "kgqs,kgqd->skd",
                probs.astype(jnp.bfloat16),
                grad_heads,
                preferred_element_type=jnp.float32,
            )
            return (dq_out, key_part, value_part)

        def backstep_passed(dq_in):
            return (dq_in, kv_zeros, kv_zeros)

        dq_next, key_part, value_part = lax.cond(
            key_first <= last_query, backstep_active, backstep_passed, dq_running
        )
        return (dq_next, (key_part, value_part))

    dq_total, kv_parts = lax.scan(backstep, dq_zeros, (key_stack, value_stack, block_numbers))
    key_terms = kv_parts[0].reshape(key_total, kv_heads, head_dim)
    value_terms = kv_parts[1].reshape(key_total, kv_heads, head_dim)
    grad_keys, grad_values = (
        lax.psum_scatter(
            key_terms.astype(jnp.bfloat16), "context", scatter_dimension=0, tiled=True
        ).astype(jnp.float32),
        lax.psum_scatter(
            value_terms.astype(jnp.bfloat16), "context", scatter_dimension=0, tiled=True
        ).astype(jnp.float32),
    )
    grad_q_normed = rotate_back(dq_total.reshape(tok_rows, q_heads, head_dim), cosine, sine)
    q_gain_part = jnp.sum(grad_q_normed * query_raw * query_scale, axis=(0, 1))
    grad_q_raw = (
        norm_backward(query_raw, query_scale, q_gain, grad_q_normed)
        .astype(jnp.bfloat16)
        .reshape(tok_rows, q_heads * head_dim)
    )
    grad_k_normed = rotate_back(grad_keys, cosine, sine)
    k_gain_part = jnp.sum(grad_k_normed * unnormed_key * key_scale, axis=(0, 1))
    grad_k_raw = (
        norm_backward(unnormed_key, key_scale, k_gain, grad_k_normed)
        .astype(jnp.bfloat16)
        .reshape(tok_rows, kv_heads * head_dim)
    )
    grad_v_low = grad_values.astype(jnp.bfloat16).reshape(tok_rows, kv_heads * head_dim)
    query_grad = jnp.einsum(
        "td,th->dh", first_normed, grad_q_raw, preferred_element_type=jnp.float32
    )
    key_grad = jnp.einsum("td,th->dh", first_normed, grad_k_raw, preferred_element_type=jnp.float32)
    value_grad = jnp.einsum(
        "td,th->dh", first_normed, grad_v_low, preferred_element_type=jnp.float32
    )
    grad_normed_one = jnp.einsum(
        "th,dh->td", grad_q_raw, q_full, preferred_element_type=jnp.float32
    )
    grad_normed_one = grad_normed_one + jnp.einsum(
        "th,dh->td", grad_k_raw, k_full, preferred_element_type=jnp.float32
    )
    grad_normed_one = grad_normed_one + jnp.einsum(
        "th,dh->td", grad_v_low, v_full, preferred_element_type=jnp.float32
    )
    grad_normed_one = lax.psum(grad_normed_one.astype(jnp.bfloat16), "tensor").astype(jnp.float32)
    attn_gain_part = jnp.sum(grad_normed_one * residual_in * scale_one, axis=0)
    input_grad = grad_mixed + norm_backward(residual_in, scale_one, attn_gain, grad_normed_one)
    share = 1.0 / lax.axis_size("tensor")
    attn_gain_grad, q_gain_grad, k_gain_grad, ffn_gain_grad = lax.psum(
        (attn_gain_part * share, q_gain_part, k_gain_part, ffn_gain_part * share),
        ("fsdp", "context", "tensor"),
    )
    shares = (
        lax.psum_scatter(
            query_grad.astype(jnp.bfloat16), "fsdp", scatter_dimension=0, tiled=True
        ).astype(jnp.float32),
        lax.psum_scatter(
            key_grad.astype(jnp.bfloat16), "fsdp", scatter_dimension=0, tiled=True
        ).astype(jnp.float32),
        lax.psum_scatter(
            value_grad.astype(jnp.bfloat16), "fsdp", scatter_dimension=0, tiled=True
        ).astype(jnp.float32),
        lax.psum_scatter(
            out_proj_grad.astype(jnp.bfloat16), "fsdp", scatter_dimension=1, tiled=True
        ).astype(jnp.float32),
        lax.psum_scatter(
            gate_grad.astype(jnp.bfloat16), "fsdp", scatter_dimension=0, tiled=True
        ).astype(jnp.float32),
        lax.psum_scatter(
            up_grad.astype(jnp.bfloat16), "fsdp", scatter_dimension=0, tiled=True
        ).astype(jnp.float32),
        lax.psum_scatter(
            down_grad.astype(jnp.bfloat16), "fsdp", scatter_dimension=1, tiled=True
        ).astype(jnp.float32),
    )
    weight_grads = (
        lax.psum(shares[0].astype(jnp.bfloat16), "context").astype(jnp.float32),
        lax.psum(shares[1].astype(jnp.bfloat16), "context").astype(jnp.float32),
        lax.psum(shares[2].astype(jnp.bfloat16), "context").astype(jnp.float32),
        lax.psum(shares[3].astype(jnp.bfloat16), "context").astype(jnp.float32),
        lax.psum(shares[4].astype(jnp.bfloat16), "context").astype(jnp.float32),
        lax.psum(shares[5].astype(jnp.bfloat16), "context").astype(jnp.float32),
        lax.psum(shares[6].astype(jnp.bfloat16), "context").astype(jnp.float32),
    )
    return (
        block_out,
        input_grad,
        attn_gain_grad,
        q_gain_grad,
        k_gain_grad,
        weight_grads[0],
        weight_grads[1],
        weight_grads[2],
        weight_grads[3],
        ffn_gain_grad,
        weight_grads[4],
        weight_grads[5],
        weight_grads[6],
    )


def solution(mesh):
    in_specs = (
        P(("fsdp", "context"), None),
        P(("fsdp", "context"), None),
        P("fsdp", None),
        P(),
        P(),
        P(),
        P("fsdp", "tensor"),
        P("fsdp", "tensor"),
        P("fsdp", "tensor"),
        P("tensor", "fsdp"),
        P(),
        P("fsdp", "tensor"),
        P("fsdp", "tensor"),
        P("tensor", "fsdp"),
    )
    out_specs = (
        P(("fsdp", "context"), None),
        P(("fsdp", "context"), None),
        P(),
        P(),
        P(),
        P("fsdp", "tensor"),
        P("fsdp", "tensor"),
        P("fsdp", "tensor"),
        P("tensor", "fsdp"),
        P(),
        P("fsdp", "tensor"),
        P("fsdp", "tensor"),
        P("tensor", "fsdp"),
    )
    return jax.shard_map(
        on_device, mesh=mesh, in_specs=in_specs, out_specs=out_specs, check_vma=False
    )
```

profile of v0, /device:TPU:0, one launch (start us, length us, event | category | flops | bytes accessed | tf_op | source)
XLA Modules:
  0.0 785.9 jit_solution(5082527310274687260)
XLA Ops:
  13.9 24.0 %all_gather.29 = bf16[1024,256]{1,0:T(8,128)(2,1)S(1)} all-gather(bf16[256,256]{1,0:T(8,128)(2,1)S(1)} %copy-done.39), channel_id=1, replica_groups=mesh['fsdp'=4,'context'=2,'tensor'=4] {'fsdp'}, dimensions={0}, use_global_device_ids=true | all-gather | bytes 655360 | tf_op jit(solution)/shard_map/all_gather | solution.py:72
  37.9 19.6 %all_gather.32 = bf16[1024,256]{1,0:T(8,128)(2,1)S(1)} all-gather(bf16[256,256]{1,0:T(8,128)(2,1)S(1)} %copy-done.40), channel_id=1, replica_groups=mesh['fsdp'=4,'context'=2,'tensor'=4] {'fsdp'}, dimensions={0}, use_global_device_ids=true | all-gather | bytes 655360 | tf_op jit(solution)/shard_map/all_gather | solution.py:73
  62.5 10.2 %all_gather.33 = bf16[1536,2,128]{2,0,1:T(8,128)(2,1)} all-gather(bf16[768,2,128]{2,0,1:T(8,128)(2,1)} %copy.106), channel_id=1, replica_groups=mesh['fsdp'=4,'context'=2,'tensor'=4] {'context'}, dimensions={0}, use_global_device_ids=true | all-gather | bytes 1179648 | tf_op jit(solution)/shard_map/all_gather | solution.py:142
  78.0 8.6 %all_gather.30 = bf16[1536,2,128]{2,0,1:T(8,128)(2,1)} all-gather(bf16[768,2,128]{2,0,1:T(8,128)(2,1)S(1)} %pad_maximum_fusion.3), channel_id=1, replica_groups=mesh['fsdp'=4,'context'=2,'tensor'=4] {'context'}, dimensions={0}, use_global_device_ids=true | all-gather | bytes 1179648 | tf_op jit(solution)/shard_map/all_gather | solution.py:138
  98.5 13.5 %while.33 = (s32[]{:T(128)}, f32[2,2,768]{2,1,0:T(2,128)S(1)}, f32[2,2,768]{2,1,0:T(2,128)S(1)}, f32[2,2,768,128]{3,2,1,0:T(8,128)}, s32[2]{0:T(128)S(1)}, /*ind...) while((s32[]{:T(128)}, f32[2,2,768]{2,1,0:T(2,128)S(1)}, ...), condition=%wide.region_13.14_spmd.clone, body=%wide.region_6.13_spmd.clone.sunk | while | flops 1241202432 | bytes 51345888 | solution.py:158
  100.0 10.8 %conditional.6 = ((f32[2,2,768]{2,1,0:T(2,128)S(1)}, f32[2,2,768]{2,1,0:T(2,128)S(1)}, f32[2,2,768,128]{3,2,1,0:T(8,128)})) conditional(s32[]{:T(128)} %convert_element_type.381, (f32[2,2,768]{2,1,0:T(2,128)S(1)}, f32[2,2,768]{2,1,0:T(2,128)S(1)}, f32[2,2,768,128]{3,2,1,0:T(8,128)}) %tuple.111, (s32[]{:T(128)}, s32[]{:T(128)}, s32[4]{0:T(128)}, ...), branch_computations={%region_7.7_spmd, %region_8.12_spmd} | conditional | flops 1241202432 | bytes 51342520 | solution.py:156
  123.9 50.1 %all-reduce.8.cloned.1.call-done = bf16[768,1024]{1,0:T(8,128)(2,1)} async-done(((bf16[768,1024]{1,0:T(8,128)(2,1)}), bf16[768,1024]{1,0:T(8,128)(2,1)}) %all-reduce.8.cloned.1.call-update) | async-done | bytes 1572880 | tf_op jit(solution)/shard_map/psum | solution.py:167
  177.9 34.7 %all-gather.12.cloned.1.call-done = bf16[1024,768]{1,0:T(8,128)(2,1)} async-done(((bf16[256,768]{1,0:T(8,128)(2,1)}), bf16[1024,768]{1,0:T(8,128)(2,1)}) %all-gather.12.cloned.1.call-update) | async-done | bytes 1572880 | tf_op jit(solution)/shard_map/all_gather | solution.py:174
  212.6 4.6 fusion.86
  217.3 32.8 %all-gather.10.cloned.1.call-done = bf16[1024,768]{1,0:T(8,128)(2,1)} async-done(((bf16[256,768]{1,0:T(8,128)(2,1)}), bf16[1024,768]{1,0:T(8,128)(2,1)}) %all-gather.10.cloned.1.call-update) | async-done | bytes 1572880 | tf_op jit(solution)/shard_map/all_gather | solution.py:173
  250.0 4.7 fusion.85
  254.7 33.4 %all-gather.14.cloned.1.call-done = bf16[768,1024]{1,0:T(8,128)(2,1)} async-done(((bf16[768,256]{1,0:T(8,128)(2,1)}), bf16[768,1024]{1,0:T(8,128)(2,1)}) %all-gather.14.cloned.1.call-update) | async-done | bytes 1572880 | tf_op jit(solution)/shard_map/all_gather | solution.py:175
  288.0 6.6 multiply_convert_fusion.1
  300.2 40.6 %all-reduce.10.cloned.1.call-done = bf16[768,1024]{1,0:T(8,128)(2,1)} async-done(((bf16[768,1024]{1,0:T(8,128)(2,1)}), bf16[768,1024]{1,0:T(8,128)(2,1)}) %all-reduce.10.cloned.1.call-update) | async-done | bytes 1572880 | tf_op jit(solution)/shard_map/psum | solution.py:201
  348.8 22.8 %while.34 = (s32[]{:T(128)}, f32[768,2,2,128]{3,0,2,1:T(8,128)S(1)}, bf16[2,768,2,128]{3,1,0,2:T(8,128)(2,1)}, bf16[2,768,2,128]{3,1,0,2:T(8,128)(2,1)}, s32[2]{...) while((s32[]{:T(128)}, ...), condition=%wide.region_25.26_spmd.clone, body=%wide.region_20.25_spmd.clone.sunk | while | flops 3046450944 | bytes 66817592 | solution.py:270
  350.8 13.9 %conditional.7 = (f32[768,2,2,128]{3,0,2,1:T(8,128)S(1)}, bf16[1,768,2,128]{3,1,2,0:T(8,128)(2,1)}, bf16[1,768,2,128]{3,1,2,0:T(8,128)(2,1)S(1)}) conditional(s32[]{:T(128)} %convert_element_type.382, f32[768,2,2,128]{3,0,2,1:T(8,128)S(1)} %get-tuple-element.916, (s32[]{:T(128)}, s32[]{:T(128)}, s32[4]{0:T(128)}, s32[768]{0:T(1024)S(1)}, ...), branch_computations={%region_21.21_spmd, %region_22.24_spmd} | conditional | flops 3046450944 | bytes 65240836 | solution.py:265
  389.4 4.6 convolution_convert_fusion.1
  394.1 4.3 convolution_convert_fusion.3
  398.5 4.3 convolution_convert_fusion.2
  403.5 4.3 convolution_convert_fusion.4
  410.7 12.0 %reduce-scatter.10.cloned.1.call-done = bf16[768,2,128]{2,0,1:T(8,128)(2,1)} async-done(((bf16[1536,2,128]{2,0,1:T(8,128)(2,1)}), bf16[768,2,128]{2,0,1:T(8,128)(2,1)}) %reduce-scatter.10.cloned.1.call-update) | async-done | bytes 393232 | tf_op jit(solution)/shard_map/reduce_scatter | solution.py:274
  438.5 13.6 %reduce-scatter.20.cloned.1.call-done = bf16[512,256]{1,0:T(8,128)(2,1)} async-done(((bf16[512,1024]{1,0:T(8,128)(2,1)}), bf16[512,256]{1,0:T(8,128)(2,1)}) %reduce-scatter.20.cloned.1.call-update) | async-done | bytes 262160 | tf_op jit(solution)/shard_map/reduce_scatter | solution.py:330
  452.1 28.2 %reduce-scatter.14.cloned.1.call-done = bf16[256,512]{1,0:T(8,128)(2,1)} async-done(((bf16[1024,512]{1,0:T(8,128)(2,1)}), bf16[256,512]{1,0:T(8,128)(2,1)}) %reduce-scatter.14.cloned.1.call-update) | async-done | bytes 262160 | tf_op jit(solution)/shard_map/reduce_scatter | solution.py:321
  480.3 36.1 %reduce-scatter.26.cloned.1.call-done = bf16[768,256]{1,0:T(8,128)(2,1)} async-done(((bf16[768,1024]{1,0:T(8,128)(2,1)}), bf16[768,256]{1,0:T(8,128)(2,1)}) %reduce-scatter.26.cloned.1.call-update) | async-done | bytes 393232 | tf_op jit(solution)/shard_map/reduce_scatter | solution.py:339
  516.4 36.6 %reduce-scatter.22.cloned.1.call-done = bf16[256,768]{1,0:T(8,128)(2,1)} async-done(((bf16[1024,768]{1,0:T(8,128)(2,1)}), bf16[256,768]{1,0:T(8,128)(2,1)}) %reduce-scatter.22.cloned.1.call-update) | async-done | bytes 393232 | tf_op jit(solution)/shard_map/reduce_scatter | solution.py:333
  553.0 36.4 %reduce-scatter.24.cloned.1.call-done = bf16[256,768]{1,0:T(8,128)(2,1)} async-done(((bf16[1024,768]{1,0:T(8,128)(2,1)}), bf16[256,768]{1,0:T(8,128)(2,1)}) %reduce-scatter.24.cloned.1.call-update) | async-done | bytes 393232 | tf_op jit(solution)/shard_map/reduce_scatter | solution.py:336
  589.5 22.7 %reduce-scatter.18.cloned.1.call-done = bf16[256,256]{1,0:T(8,128)(2,1)} async-done(((bf16[1024,256]{1,0:T(8,128)(2,1)}), bf16[256,256]{1,0:T(8,128)(2,1)}) %reduce-scatter.18.cloned.1.call-update) | async-done | bytes 131088 | tf_op jit(solution)/shard_map/reduce_scatter | solution.py:327
  612.2 22.7 %reduce-scatter.16.cloned.1.call-done = bf16[256,256]{1,0:T(8,128)(2,1)} async-done(((bf16[1024,256]{1,0:T(8,128)(2,1)}), bf16[256,256]{1,0:T(8,128)(2,1)}) %reduce-scatter.16.cloned.1.call-update) | async-done | bytes 131088 | tf_op jit(solution)/shard_map/reduce_scatter | solution.py:324
  634.9 69.7 %all-reduce.12.cloned.1.call-done = (bf16[768,1024]{1,0:T(8,128)(2,1)}, bf16[768,1024]{1,0:T(8,128)(2,1)}) async-done(((bf16[768,1024]{1,0:T(8,128)(2,1)}, bf16[768,1024]{1,0:T(8,128)(2,1)}), (bf16[768,1024]{1,0:T(8,128)(2,1)}, bf16[768,1024]{1,0:T(8,128)(2,1)})) %all-reduce.12.cloned.1.call-update) | async-done | bytes 3145744 | tf_op jit(solution)/shard_map/psum | solution.py:184
  707.4 39.9 %all-reduce = (f32[1024]{0:T(1024)}, f32[128]{0:T(128)}, f32[128]{0:T(128)}, f32[1024]{0:T(1024)}) all-reduce(f32[1024]{0:T(1024)S(1)} %get-tuple-element.663, f32[128]{0:T(128)S(1)} %bitcast_reduce_fusion, f32[128]{0:T(128)S(1)} %bitcast_reduce_fusion.1, ...), channel_id=1, replica_groups=mesh['fsdp'=4,'context'=2,'tensor'=4] {'fsdp','context','tensor'}, use_global_device_ids=true, to_apply=%region_33.34 | all-reduce | flops 2304 | bytes 18432 | tf_op jit(solution)/shard_map/psum | solution.py:316
  747.3 5.0 fusion.50
  752.3 16.5 %all-reduce.14.cloned.1.call-done = (bf16[256,512]{1,0:T(8,128)(2,1)}, bf16[256,256]{1,0:T(8,128)(2,1)}, bf16[256,256]{1,0:T(8,128)(2,1)}, bf16[512,256]{1,0:T(8...) async-done(((bf16[256,512]{1,0:T(8,128)(2,1)}, bf16[256,256]{1,0:T(8,128)(2,1)}, bf16[256,256]{1,0:T(8,128)(2,1)}, ...) | async-done | bytes 1966096 | tf_op jit(solution)/shard_map/psum | solution.py:344
  (287 shorter events, 141.1 us)
Async XLA Ops:
  7.2 30.7 %copy-start.40 = (bf16[256,256]{1,0:T(8,128)(2,1)S(1)}, bf16[256,256]{1,0:T(8,128)(2,1)}, u32[]{:S(2)}) copy-start(bf16[256,256]{1,0:T(8,128)(2,1)} %param.30) | copy-start | bytes 393220
  7.2 81.6 %all-gather.6.cloned.1.call-start = ((), (), s32[]{:S(2)}) async-start(), calls=%async_computation.9 | async-start | bytes 1310720 | tf_op jit(solution)/shard_map/all_gather | solution.py:71
  7.9 50.4 %copy-start = (bf16[768,1024]{1,0:T(8,128)(2,1)S(1)}, bf16[768,1024]{1,0:T(8,128)(2,1)}, u32[]{:S(2)}) copy-start(bf16[768,1024]{1,0:T(8,128)(2,1)} %param.22) | copy-start | bytes 4718596
  7.9 110.1 %all-gather.8.cloned.1.call-start = ((), (), s32[]{:S(2)}) async-start(), calls=%async_computation.10 | async-start | bytes 1310720 | tf_op jit(solution)/shard_map/all_gather | solution.py:74
  8.7 165.3 %all-reduce.8.cloned.1.call-start = ((), (), s32[]{:S(2)}) async-start(), calls=%async_computation.11 | async-start | bytes 3145728 | tf_op jit(solution)/shard_map/psum | solution.py:167
  12.7 76.1 %copy-start.47 = (f32[768]{0:T(1024)}, f32[768]{0:T(1024)S(1)}, u32[]{:S(2)}) copy-start(f32[768]{0:T(1024)S(1)} %get-tuple-element.653) | copy-start | bytes 9220
  13.5 79.3 %copy-start.21 = (f32[768,64]{0,1:T(8,128)}, f32[768,64]{0,1:T(8,128)S(1)}, u32[]{:S(2)}) copy-start(f32[768,64]{0,1:T(8,128)S(1)} %get-tuple-element.650) | copy-start | bytes 589828
  13.5 79.3 %copy-start.23 = (f32[768,64]{0,1:T(8,128)}, f32[768,64]{0,1:T(8,128)S(1)}, u32[]{:S(2)}) copy-start(f32[768,64]{0,1:T(8,128)S(1)} %get-tuple-element.651) | copy-start | bytes 589828
  13.7 63.7 %copy-start.17 = (f32[768,64]{1,0:T(8,128)}, f32[768,64]{1,0:T(8,128)S(1)}, u32[]{:S(2)}) copy-start(f32[768,64]{1,0:T(8,128)S(1)} %copy.102) | copy-start | bytes 589828
  13.9 63.5 %copy-start.19 = (f32[768,64]{1,0:T(8,128)}, f32[768,64]{1,0:T(8,128)S(1)}, u32[]{:S(2)}) copy-start(f32[768,64]{1,0:T(8,128)S(1)} %copy.103) | copy-start | bytes 589828
  37.9 34.8 %copy-start.27 = (bf16[1024,256]{1,0:T(8,128)(2,1)}, bf16[1024,256]{1,0:T(8,128)(2,1)S(1)}, u32[]{:S(2)}) copy-start(bf16[1024,256]{1,0:T(8,128)(2,1)S(1)} %all_gather.29) | copy-start | bytes 1572868
  121.7 54.5 %copy-start.46 = (f32[1024]{0:T(1024)S(1)}, f32[1024]{0:T(1024)}, u32[]{:S(2)}) copy-start(f32[1024]{0:T(1024)} %param.32) | copy-start | bytes 12292
  121.7 90.9 %all-gather.12.cloned.1.call-start = ((), (), s32[]{:S(2)}) async-start(), calls=%async_computation.13 | async-start | bytes 1966080 | tf_op jit(solution)/shard_map/all_gather | solution.py:174
  122.3 127.8 %all-gather.10.cloned.1.call-start = ((), (), s32[]{:S(2)}) async-start(), calls=%async_computation.12 | async-start | bytes 1966080 | tf_op jit(solution)/shard_map/all_gather | solution.py:173
  122.9 165.2 %all-gather.14.cloned.1.call-start = ((), (), s32[]{:S(2)}) async-start(), calls=%async_computation.14 | async-start | bytes 1966080 | tf_op jit(solution)/shard_map/all_gather | solution.py:175
  123.4 217.3 %all-reduce.10.cloned.1.call-start = ((), (), s32[]{:S(2)}) async-start(), calls=%async_computation.15 | async-start | bytes 3145728 | tf_op jit(solution)/shard_map/psum | solution.py:201
  299.5 108.3 %reduce-scatter.12.cloned.1.call-start = ((), (), s32[]{:S(2)}) async-start(), calls=%async_computation.17 | async-start | bytes 1179648 | tf_op jit(solution)/shard_map/reduce_scatter | solution.py:277
  371.6 51.1 %reduce-scatter.10.cloned.1.call-start = ((), (), s32[]{:S(2)}) async-start(), calls=%async_computation.16 | async-start | bytes 1179648 | tf_op jit(solution)/shard_map/reduce_scatter | solution.py:274
  372.4 79.7 %reduce-scatter.20.cloned.1.call-start = ((), (), s32[]{:S(2)}) async-start(), calls=%async_computation.21 | async-start | bytes 1310720 | tf_op jit(solution)/shard_map/reduce_scatter | solution.py:330
  376.6 103.7 %reduce-scatter.14.cloned.1.call-start = ((), (), s32[]{:S(2)}) async-start(), calls=%async_computation.18 | async-start | bytes 1310720 | tf_op jit(solution)/shard_map/reduce_scatter | solution.py:321
  389.4 127.0 %reduce-scatter.26.cloned.1.call-start = ((), (), s32[]{:S(2)}) async-start(), calls=%async_computation.24 | async-start | bytes 1966080 | tf_op jit(solution)/shard_map/reduce_scatter | solution.py:339
  394.0 159.0 %reduce-scatter.22.cloned.1.call-start = ((), (), s32[]{:S(2)}) async-start(), calls=%async_computation.22 | async-start | bytes 1966080 | tf_op jit(solution)/shard_map/reduce_scatter | solution.py:333
  398.5 191.0 %reduce-scatter.24.cloned.1.call-start = ((), (), s32[]{:S(2)}) async-start(), calls=%async_computation.23 | async-start | bytes 1966080 | tf_op jit(solution)/shard_map/reduce_scatter | solution.py:336
  402.9 209.3 %reduce-scatter.18.cloned.1.call-start = ((), (), s32[]{:S(2)}) async-start(), calls=%async_computation.20 | async-start | bytes 655360 | tf_op jit(solution)/shard_map/reduce_scatter | solution.py:327
  410.7 224.2 %reduce-scatter.16.cloned.1.call-start = ((), (), s32[]{:S(2)}) async-start(), calls=%async_computation.19 | async-start | bytes 655360 | tf_op jit(solution)/shard_map/reduce_scatter | solution.py:324
  432.9 271.8 %all-reduce.12.cloned.1.call-start = ((), (), s32[]{:S(2)}) async-start(), calls=%async_computation.25 | async-start | bytes 6291456 | tf_op jit(solution)/shard_map/psum | solution.py:184
  438.4 196.5 %copy-start.56 = (f32[512]{0:T(512)S(1)}, f32[512]{0:T(512)}, u32[]{:S(2)}) copy-start(f32[512]{0:T(512)} %get-tuple-element.628) | copy-start | bytes 6148
  438.4 196.5 %copy-start.60 = (f32[256]{0:T(256)S(1)}, f32[256]{0:T(256)}, u32[]{:S(2)}) copy-start(f32[256]{0:T(256)} %get-tuple-element.634) | copy-start | bytes 3076
  438.4 266.3 %copy-start.52 = (f32[1024]{0:T(1024)S(1)}, f32[1024]{0:T(1024)}, u32[]{:S(2)}) copy-start(f32[1024]{0:T(1024)} %param.25) | copy-start | bytes 12292
  438.4 330.4 %all-reduce.14.cloned.1.call-start = ((), (), s32[]{:S(2)}) async-start(), calls=%async_computation.26 | async-start | bytes 3932160 | tf_op jit(solution)/shard_map/psum | solution.py:344
  634.9 112.4 %copy-start.3 = (bf16[768,1024]{1,0:T(8,128)(2,1)S(1)}, bf16[768,1024]{1,0:T(8,128)(2,1)}, u32[]{:S(2)}) copy-start(bf16[768,1024]{1,0:T(8,128)(2,1)} %all-reduce.8.cloned.1.call-done) | copy-start | bytes 4718596
  634.9 112.4 %copy-start.53 = (f32[768]{0:T(1024)S(1)}, f32[768]{0:T(1024)}, u32[]{:S(2)}) copy-start(f32[768]{0:T(1024)} %get-tuple-element.652) | copy-start | bytes 9220
  (51 other events, 198.4 us)
Sparse Core Ops, SparseCore 0:
  9.6 41.4 all-gather.5
  52.6 30.8 all-gather.7
  121.8 52.1 all-reduce.7
  175.4 37.1 all-gather.11
  214.0 35.9 all-gather.9
  251.4 36.5 all-gather.13
  299.6 41.0 all-reduce.9
  371.8 30.5 reduce-scatter.11
  405.3 17.4 reduce-scatter.9
  424.9 27.1 reduce-scatter.19
  454.5 25.7 reduce-scatter.13
  482.5 33.9 reduce-scatter.25
  518.7 34.2 reduce-scatter.21
  555.2 34.2 reduce-scatter.23
  591.6 20.5 reduce-scatter.17
  614.9 19.9 reduce-scatter.15
  637.7 66.9 all-reduce.11
  707.2 61.5 all-reduce.13
where the time goes:
time: 793 us; the launch traced here: 786 us
  waiting for transfers between devices  490 us (62%)
  blocking collectives  102 us (13%)
  matrix products  82.3 us (10%)
  other arithmetic  53.4 us (7%)
  local copies, waits for them, and re-layouts  37.6 us (5%)
  between operations  15.5 us (2%)
    psum x1, waiting for transfers between devices, on_device(): lax.psum(jnp.dot(activated, d_full, preferred_element_type=jnp.float32).a...  69.7 us
    psum x1, waiting for transfers between devices, on_device(): lax.psum(jnp.dot(attention_result, o_full, preferred_element_type=jnp.flo...  50.1 us
    psum x1, waiting for transfers between devices, on_device(): lax.psum(grad_normed_two.astype(jnp.bfloat16), 'tensor').astype(jnp.float32)  40.6 us
    psum x1, blocking collectives, on_device(): lax.psum((attn_gain_part * share, q_gain_part, k_gain_part, ffn_gain_part...  39.9 us
    reduce_scatter x1, waiting for transfers between devices, on_device(): lax.psum_scatter(gate_grad.astype(jnp.bfloat16), 'fsdp', scatter_dimensio...  36.6 us
    reduce_scatter x1, waiting for transfers between devices, on_device(): lax.psum_scatter(up_grad.astype(jnp.bfloat16), 'fsdp', scatter_dimension=...  36.4 us
    reduce_scatter x1, waiting for transfers between devices, on_device(): lax.psum_scatter(down_grad.astype(jnp.bfloat16), 'fsdp', scatter_dimensio...  36.1 us
    all_gather x1, waiting for transfers between devices, on_device(): lax.all_gather(w_up, 'fsdp', axis=0, tiled=True)  34.7 us
  transfers between devices with their start and end apart: 18, of which 15 were waited for; matrix products, arithmetic and copies ran while one was open for 15% of the time, Pallas kernels for 0%

commit v1 on v0

v1 whole, which is shorter than its diff:
```python
import math

import jax
import jax.numpy as jnp
from jax import lax
from jax.sharding import PartitionSpec as P

epsilon = 1e-06
rope_base = 1000000.0
masked_score = -1e30


def inverse_rms(values):
    return lax.rsqrt(jnp.mean(values * values, axis=-1, keepdims=True) + epsilon)


def norm_backward(values, scaling, gain, grads):
    scaled = gain * grads
    cubed = scaling * scaling * scaling
    return scaling * scaled - values * cubed * jnp.mean(scaled * values, axis=-1, keepdims=True)


def doc_layout(lengths_row, positions):
    doc_ends = jnp.cumsum(lengths_row)
    doc_starts = doc_ends - lengths_row
    after_end = positions[:, None] >= doc_ends[None, :]
    inside = (positions[:, None] >= doc_starts[None, :]) & jnp.logical_not(after_end)
    packed_documents = jnp.sum(after_end.astype(jnp.int32), axis=1)
    doc_begin = jnp.sum(jnp.where(inside, doc_starts[None, :], 0), axis=1)
    return (packed_documents, positions - doc_begin)


def rope_tables(positions, head_dim):
    half_dim = head_dim // 2
    freqs = rope_base ** (-(jnp.arange(half_dim, dtype=jnp.float32) * (2.0 / head_dim)))
    angles = positions.astype(jnp.float32)[:, None] * freqs[None, :]
    return (jnp.cos(angles)[:, None, :], jnp.sin(angles)[:, None, :])


def rotate(values, cosine, sine):
    half_dim = values.shape[-1] // 2
    lower, upper = (values[..., :half_dim], values[..., half_dim:])
    return jnp.concatenate([lower * cosine - upper * sine, upper * cosine + lower * sine], axis=-1)


def rotate_back(grads, cosine, sine):
    half_dim = grads.shape[-1] // 2
    lower, upper = (grads[..., :half_dim], grads[..., half_dim:])
    return jnp.concatenate([lower * cosine + upper * sine, upper * cosine - lower * sine], axis=-1)


def flip(values, axis_name, bit):
    size = lax.axis_size(axis_name)
    return lax.ppermute(values, axis_name, [(i, i ^ bit) for i in range(size)])


def is_power(size):
    return size & (size - 1) == 0


def has_pairs():
    return lax.axis_size("context") == 2 and is_power(lax.axis_size("fsdp"))


def order_matrix(width):
    size = lax.axis_size("fsdp")
    me, side = lax.axis_index("fsdp"), lax.axis_index("context")
    piece = width // (2 * size)
    column = jnp.arange(width, dtype=jnp.int32)
    chunk = column // piece
    source = ((me ^ (chunk % size)) * 2 + (side ^ (chunk // size))) * piece + column % piece
    return column[:, None] == source[None, :]


def permute(values, spec):
    if not has_pairs():
        return values
    order = order_matrix(values.shape[-1])
    if values.ndim == 1:
        return jnp.einsum(
            spec, values[None], order.astype(jnp.float32), precision=lax.Precision.HIGHEST
        )[0]
    order = order.astype(jnp.bfloat16)
    high = values.astype(jnp.bfloat16)
    out = jnp.einsum(spec, high, order, preferred_element_type=jnp.float32)
    if values.dtype == jnp.float32:
        low = (values - high.astype(jnp.float32)).astype(jnp.bfloat16)
        out = out + jnp.einsum(spec, low, order, preferred_element_type=jnp.float32)
    return out.astype(values.dtype)


def arrange(values):
    return permute(values, "tr,rc->tc")


def restore(values):
    return permute(values, "tc,rc->tr")


def gather_weight(shard, dim):
    if not has_pairs():
        return lax.all_gather(shard, "fsdp", axis=dim, tiled=True)
    size, side = lax.axis_size("fsdp"), lax.axis_index("context")
    half = shard.shape[dim] // 2
    mine = lax.dynamic_slice_in_dim(shard, side * half, half, dim)
    rest = lax.dynamic_slice_in_dim(shard, (1 - side) * half, half, dim)
    fetched = [flip(mine, "fsdp", bit) for bit in range(1, size)]
    swapped = [flip(piece, "context", 1) for piece in fetched]
    return jnp.concatenate([mine, *fetched, rest, *swapped], axis=dim)


def scatter_grad(grad, dim):
    low = grad.astype(jnp.bfloat16)
    size = lax.axis_size("fsdp")
    if not has_pairs():
        part = lax.psum_scatter(low, "fsdp", scatter_dimension=dim, tiled=True)
        return lax.psum(part, "context").astype(jnp.float32)
    side = lax.axis_index("context")
    half = low.shape[dim] // 2
    piece = half // size
    kept = lax.slice_in_dim(low, 0, half, axis=dim)
    other = flip(lax.slice_in_dim(low, half, 2 * half, axis=dim), "context", 1)
    summed = [
        lax.slice_in_dim(kept, b * piece, (b + 1) * piece, axis=dim).astype(jnp.float32)
        + lax.slice_in_dim(other, b * piece, (b + 1) * piece, axis=dim).astype(jnp.float32)
        for b in range(size)
    ]
    arrived = [flip(summed[b].astype(jnp.bfloat16), "fsdp", b) for b in range(1, size)]
    total = summed[0]
    for part in arrived:
        total = total + part.astype(jnp.float32)
    total = total.astype(jnp.bfloat16)
    other = flip(total, "context", 1)
    first = jnp.where(side == 0, total, other)
    second = jnp.where(side == 0, other, total)
    return jnp.concatenate([first, second], axis=dim).astype(jnp.float32)


def tensor_sum(values, chunks=2):
    low = values.astype(jnp.bfloat16)
    if lax.axis_size("tensor") != 4:
        return lax.psum(low, "tensor").astype(jnp.float32)
    core = lax.axis_index("tensor") % 2
    rows, width = low.shape
    half = rows // (2 * chunks)
    pieces = low.reshape(chunks, 2, half, width)
    done = []
    for chunk in range(chunks):
        kept = lax.dynamic_index_in_dim(pieces[chunk], core, 0, keepdims=False)
        sent = lax.dynamic_index_in_dim(pieces[chunk], 1 - core, 0, keepdims=False)
        other = flip(sent, "tensor", 1)
        pair = (kept.astype(jnp.float32) + other.astype(jnp.float32)).astype(jnp.bfloat16)
        far = flip(pair, "tensor", 2)
        total = (pair.astype(jnp.float32) + far.astype(jnp.float32)).astype(jnp.bfloat16)
        other = flip(total, "tensor", 1)
        done.append(jnp.where(core == 0, total, other))
        done.append(jnp.where(core == 0, other, total))
    return jnp.concatenate(done, axis=0).astype(jnp.float32)


def sum_everywhere(values):
    for name in ("tensor", "fsdp", "context"):
        size = lax.axis_size(name)
        if is_power(size):
            bit = 1
            while bit < size:
                values = values + flip(values, name, bit)
                bit *= 2
        else:
            values = lax.psum(values, name)
    return values


def on_device(
    hidden_in,
    out_grad,
    doc_lengths,
    attn_gain,
    q_gain,
    k_gain,
    w_query,
    key_projection,
    value_projection,
    w_out,
    ffn_gain,
    w_gate,
    w_up,
    w_down,
):
    hidden_in, out_grad = arrange(hidden_in), arrange(out_grad)
    attn_gain, ffn_gain = arrange(attn_gain), arrange(ffn_gain)
    tok_rows = hidden_in.shape[0]
    head_dim = q_gain.shape[0]
    q_cols, k_cols = w_query.shape[1], key_projection.shape[1]
    qkv_full = gather_weight(
        jnp.concatenate([w_query, key_projection, value_projection], axis=1), 0
    )
    qkv_full, w_out, w_gate, w_up, w_down = lax.optimization_barrier(
        (qkv_full, w_out, w_gate, w_up, w_down)
    )
    o_full = gather_weight(w_out, 1)
    gu_full = gather_weight(jnp.concatenate([w_gate, w_up], axis=1), 0)
    d_full = gather_weight(w_down, 1)
    q_heads = q_cols // head_dim
    kv_heads = k_cols // head_dim
    group_size = q_heads // kv_heads
    inv_sqrt = 1.0 / math.sqrt(head_dim)
    first_row = lax.axis_index("context") * tok_rows
    positions = first_row + jnp.arange(tok_rows, dtype=jnp.int32)
    lengths_row = doc_lengths[0]
    query_docs, query_offsets = doc_layout(lengths_row, positions)
    cosine, sine = rope_tables(query_offsets, head_dim)
    last_query = first_row + tok_rows - 1
    residual_in = hidden_in.astype(jnp.float32)
    scale_one = inverse_rms(residual_in)
    first_normed = (residual_in * scale_one * attn_gain).astype(jnp.bfloat16)
    projected = jnp.dot(first_normed, qkv_full, preferred_element_type=jnp.float32)
    query_raw = projected[:, :q_cols].reshape(tok_rows, q_heads, head_dim)
    unnormed_key = projected[:, q_cols : q_cols + k_cols].reshape(tok_rows, kv_heads, head_dim)
    values_local = (
        projected[:, q_cols + k_cols :].astype(jnp.bfloat16).reshape(tok_rows, kv_heads, head_dim)
    )
    query_scale = inverse_rms(query_raw)
    key_scale = inverse_rms(unnormed_key)
    query_rows = rotate(query_raw * query_scale * q_gain, cosine, sine).astype(jnp.bfloat16)
    keys_local = rotate(unnormed_key * key_scale * k_gain, cosine, sine).astype(jnp.bfloat16)
    grouped_q = query_rows.reshape(tok_rows, kv_heads, group_size, head_dim)

    def block_mask(key_first, key_count):
        key_places = key_first + jnp.arange(key_count, dtype=jnp.int32)
        key_docs, key_offsets = doc_layout(lengths_row, key_places)
        return (key_places[None, :] <= positions[:, None]) & (
            key_docs[None, :] == query_docs[:, None]
        )

    def attend(running, key_blk, val_blk, key_first):
        best, total, summed = running
        allowed = block_mask(key_first, key_blk.shape[0])
        scores = (
            jnp.einsum("qkgd,skd->kgqs", grouped_q, key_blk, preferred_element_type=jnp.float32)
            * inv_sqrt
        )
        scores = jnp.where(allowed, scores, masked_score)
        new_best = jnp.maximum(best, jnp.max(scores, axis=-1))
        weights = jnp.where(allowed, jnp.exp(scores - new_best[..., None]), 0.0)
        factor = jnp.exp(best - new_best)
        total = total * factor + jnp.sum(weights, axis=-1)
        summed = summed * factor[..., None] + jnp.einsum(
            "kgqs,skd->kgqd",
            weights.astype(jnp.bfloat16),
            val_blk,
            preferred_element_type=jnp.float32,
        )
        return (new_best, total, summed)

    start_state = (
        jnp.full((kv_heads, group_size, tok_rows), masked_score, jnp.float32),
        jnp.zeros((kv_heads, group_size, tok_rows), jnp.float32),
        jnp.zeros((kv_heads, group_size, tok_rows, head_dim), jnp.float32),
    )
    two_sided = lax.axis_size("context") == 2
    if two_sided:
        kv_pair = lax.ppermute(
            jnp.concatenate([keys_local, values_local], axis=1), "context", [(0, 1)]
        )
        keys_before, values_before = kv_pair[:, :kv_heads], kv_pair[:, kv_heads:]
        result = attend(start_state, keys_local, values_local, first_row)
        result = lax.cond(
            first_row > 0,
            lambda state: attend(state, keys_before, values_before, 0),
            lambda state: state,
            result,
        )
    else:
        keys_in = lax.all_gather(keys_local, "context", axis=0, tiled=True)
        key_rows = keys_in.shape[0]
        count_of_blocks = key_rows // tok_rows
        key_blocks = keys_in.reshape(count_of_blocks, tok_rows, kv_heads, head_dim)
        val_blocks = lax.all_gather(values_local, "context", axis=0, tiled=True).reshape(
            count_of_blocks, tok_rows, kv_heads, head_dim
        )

        def advance(current, inputs):
            key_blk, val_blk, number = inputs
            block_first = number * tok_rows

            def advance_active(state_in):
                return attend(state_in, key_blk, val_blk, block_first)

            def advance_passed(state_in):
                return state_in

            return (lax.cond(block_first <= last_query, advance_active, advance_passed, current), None)

        result, unused = lax.scan(
            advance, start_state, (key_blocks, val_blocks, jnp.arange(count_of_blocks, dtype=jnp.int32))
        )
    best, total, summed = result
    attn_exact = summed / total[..., None]
    log_total = best + jnp.log(total)
    attention_result = (
        attn_exact.astype(jnp.bfloat16).transpose(2, 0, 1, 3).reshape(tok_rows, q_heads * head_dim)
    )
    attn_out = tensor_sum(jnp.dot(attention_result, o_full, preferred_element_type=jnp.float32))
    mixed = residual_in + attn_out
    scale_two = inverse_rms(mixed)
    normed_two = (mixed * scale_two * ffn_gain).astype(jnp.bfloat16)
    hidden = jnp.dot(normed_two, gu_full, preferred_element_type=jnp.float32)
    gate, up_part = hidden[:, : w_gate.shape[1]], hidden[:, w_gate.shape[1] :]
    sigmoid_gate = jax.nn.sigmoid(gate)
    silu_gate = gate * sigmoid_gate
    activated = (silu_gate * up_part).astype(jnp.bfloat16)
    grad_top = out_grad.astype(jnp.float32)
    down_grad = jnp.einsum("tf,td->fd", activated, out_grad, preferred_element_type=jnp.float32)
    grad_act = jnp.einsum("td,fd->tf", out_grad, d_full, preferred_element_type=jnp.float32)
    silu_slope = sigmoid_gate * (1.0 + gate * (1.0 - sigmoid_gate))
    grad_gate = (grad_act * up_part * silu_slope).astype(jnp.bfloat16)
    grad_up = (grad_act * silu_gate).astype(jnp.bfloat16)
    grad_hidden = jnp.concatenate([grad_gate, grad_up], axis=1)
    hidden_grad = jnp.einsum("td,tf->df", normed_two, grad_hidden, preferred_element_type=jnp.float32)
    normed_two_part = jnp.einsum("tf,df->td", grad_hidden, gu_full, preferred_element_type=jnp.float32)
    down_share = scatter_grad(down_grad, 1)
    hidden_share = scatter_grad(hidden_grad, 0)
    ffn_gain_part = jnp.sum(normed_two_part * mixed * scale_two, axis=0)
    grad_normed_two = tensor_sum(normed_two_part)
    mlp_part = jnp.dot(activated, d_full, preferred_element_type=jnp.float32).astype(jnp.bfloat16)
    grad_mixed = grad_top + norm_backward(mixed, scale_two, ffn_gain, grad_normed_two)
    grad_mixed_low = grad_mixed.astype(jnp.bfloat16)
    out_proj_grad = jnp.einsum(
        "th,td->hd", attention_result, grad_mixed_low, preferred_element_type=jnp.float32
    )
    out_share = scatter_grad(out_proj_grad, 1)
    grad_heads = jnp.einsum(
        "td,hd->th", grad_mixed_low, o_full, preferred_element_type=jnp.float32
    ).astype(jnp.bfloat16)
    grad_rows = grad_heads.reshape(tok_rows, kv_heads, group_size, head_dim)
    grad_heads = grad_rows.transpose(1, 2, 0, 3)
    delta = jnp.sum(grad_heads.astype(jnp.float32) * attn_exact, axis=-1)
    def back_block(dq_in, key_blk, val_blk, key_first):
        allowed = block_mask(key_first, tok_rows)
        scores = (
            jnp.einsum("qkgd,skd->kgqs", grouped_q, key_blk, preferred_element_type=jnp.float32)
            * inv_sqrt
        )
        probs = jnp.where(allowed, jnp.exp(scores - log_total[..., None]), 0.0)
        grad_probs = jnp.einsum(
            "kgqd,skd->kgqs", grad_heads, val_blk, preferred_element_type=jnp.float32
        )
        grad_scores = (probs * (grad_probs - delta[..., None])).astype(jnp.bfloat16)
        dq_out = (
            dq_in
            + jnp.einsum(
                "kgqs,skd->qkgd", grad_scores, key_blk, preferred_element_type=jnp.float32
            )
            * inv_sqrt
        )
        key_part = (
            jnp.einsum(
                "kgqs,qkgd->skd", grad_scores, grouped_q, preferred_element_type=jnp.float32
            )
            * inv_sqrt
        )
        value_part = jnp.einsum(
            "kgqs,kgqd->skd",
            probs.astype(jnp.bfloat16),
            grad_heads,
            preferred_element_type=jnp.float32,
        )
        return (dq_out, key_part, value_part)

    kv_zeros = jnp.zeros((tok_rows, kv_heads, head_dim), jnp.float32)
    dq_zeros = jnp.zeros((tok_rows, kv_heads, group_size, head_dim), jnp.float32)
    if two_sided:
        dq_total, key_before, value_before = lax.cond(
            first_row > 0,
            lambda dq_in: back_block(dq_in, keys_before, values_before, 0),
            lambda dq_in: (dq_in, kv_zeros, kv_zeros),
            dq_zeros,
        )
        mlp_part, dq_total = lax.optimization_barrier((mlp_part, dq_total))
        kv_back = lax.ppermute(
            jnp.concatenate([key_before, value_before], axis=1).astype(jnp.bfloat16),
            "context",
            [(1, 0)],
        ).astype(jnp.float32)
        dq_total, grad_keys, grad_values = back_block(
            dq_total, keys_local, values_local, first_row
        )
        grad_keys = grad_keys + kv_back[:, :kv_heads]
        grad_values = grad_values + kv_back[:, kv_heads:]
    else:
        back_keys, back_values = (
            lax.all_gather(keys_local, "context", axis=0, tiled=True),
            lax.all_gather(values_local, "context", axis=0, tiled=True),
        )
        key_total = back_keys.shape[0]
        back_count = key_total // tok_rows
        key_stack = back_keys.reshape(back_count, tok_rows, kv_heads, head_dim)
        value_stack = back_values.reshape(back_count, tok_rows, kv_heads, head_dim)
        block_numbers = jnp.arange(back_count, dtype=jnp.int32)

        def backstep(dq_running, inputs):
            key_blk, val_blk, number = inputs
            key_first = number * tok_rows

            def backstep_active(dq_in):
                return back_block(dq_in, key_blk, val_blk, key_first)

            def backstep_passed(dq_in):
                return (dq_in, kv_zeros, kv_zeros)

            dq_next, key_part, value_part = lax.cond(
                key_first <= last_query, backstep_active, backstep_passed, dq_running
            )
            return (dq_next, (key_part, value_part))

        dq_total, kv_parts = lax.scan(backstep, dq_zeros, (key_stack, value_stack, block_numbers))
        key_terms = kv_parts[0].reshape(key_total, kv_heads, head_dim)
        value_terms = kv_parts[1].reshape(key_total, kv_heads, head_dim)
        grad_keys, grad_values = (
            lax.psum_scatter(
                key_terms.astype(jnp.bfloat16), "context", scatter_dimension=0, tiled=True
            ).astype(jnp.float32),
            lax.psum_scatter(
                value_terms.astype(jnp.bfloat16), "context", scatter_dimension=0, tiled=True
            ).astype(jnp.float32),
        )
    mlp_out = tensor_sum(mlp_part)
    block_out = (mixed + mlp_out).astype(jnp.bfloat16)
    grad_q_normed = rotate_back(dq_total.reshape(tok_rows, q_heads, head_dim), cosine, sine)
    q_gain_part = jnp.sum(grad_q_normed * query_raw * query_scale, axis=(0, 1))
    grad_q_raw = (
        norm_backward(query_raw, query_scale, q_gain, grad_q_normed)
        .astype(jnp.bfloat16)
        .reshape(tok_rows, q_heads * head_dim)
    )
    grad_k_normed = rotate_back(grad_keys, cosine, sine)
    k_gain_part = jnp.sum(grad_k_normed * unnormed_key * key_scale, axis=(0, 1))
    grad_k_raw = (
        norm_backward(unnormed_key, key_scale, k_gain, grad_k_normed)
        .astype(jnp.bfloat16)
        .reshape(tok_rows, kv_heads * head_dim)
    )
    grad_v_low = grad_values.astype(jnp.bfloat16).reshape(tok_rows, kv_heads * head_dim)
    grad_kv = jnp.concatenate([grad_k_raw, grad_v_low], axis=1)
    query_grad = jnp.einsum(
        "td,th->dh", first_normed, grad_q_raw, preferred_element_type=jnp.float32
    )
    kv_grad = jnp.einsum("td,th->dh", first_normed, grad_kv, preferred_element_type=jnp.float32)
    query_share = scatter_grad(query_grad, 0)
    kv_share = scatter_grad(kv_grad, 0)
    normed_one_part = jnp.einsum(
        "th,dh->td",
        jnp.concatenate([grad_q_raw, grad_kv], axis=1),
        qkv_full,
        preferred_element_type=jnp.float32,
    )
    attn_gain_part = jnp.sum(normed_one_part * residual_in * scale_one, axis=0)
    grad_normed_one = tensor_sum(normed_one_part)
    input_grad = grad_mixed + norm_backward(residual_in, scale_one, attn_gain, grad_normed_one)
    gains = sum_everywhere(
        jnp.concatenate(
            [restore(attn_gain_part), restore(ffn_gain_part), q_gain_part, k_gain_part]
        )
    )
    width = attn_gain.shape[0]
    attn_gain_grad, ffn_gain_grad = gains[:width], gains[width : 2 * width]
    q_gain_grad = gains[2 * width : 2 * width + head_dim]
    k_gain_grad = gains[2 * width + head_dim :]
    weight_grads = (
        query_share,
        kv_share[:, :k_cols],
        kv_share[:, k_cols:],
        out_share,
        hidden_share[:, : w_gate.shape[1]],
        hidden_share[:, w_gate.shape[1] :],
        down_share,
    )
    return (
        restore(block_out),
        restore(input_grad),
        attn_gain_grad,
        q_gain_grad,
        k_gain_grad,
        weight_grads[0],
        weight_grads[1],
        weight_grads[2],
        weight_grads[3],
        ffn_gain_grad,
        weight_grads[4],
        weight_grads[5],
        weight_grads[6],
    )


def solution(mesh):
    in_specs = (
        P(("fsdp", "context"), None),
        P(("fsdp", "context"), None),
        P("fsdp", None),
        P(),
        P(),
        P(),
        P("fsdp", "tensor"),
        P("fsdp", "tensor"),
        P("fsdp", "tensor"),
        P("tensor", "fsdp"),
        P(),
        P("fsdp", "tensor"),
        P("fsdp", "tensor"),
        P("tensor", "fsdp"),
    )
    out_specs = (
        P(("fsdp", "context"), None),
        P(("fsdp", "context"), None),
        P(),
        P(),
        P(),
        P("fsdp", "tensor"),
        P("fsdp", "tensor"),
        P("fsdp", "tensor"),
        P("tensor", "fsdp"),
        P(),
        P("fsdp", "tensor"),
        P("fsdp", "tensor"),
        P("tensor", "fsdp"),
    )
    return jax.shard_map(
        on_device, mesh=mesh, in_specs=in_specs, out_specs=out_specs, check_vma=False
    )
```

time: 793 us -> 576 us (0.73)
  waiting for transfers between devices: 490 us -> 111 us
  starting transfers between devices: 1.59 us -> 129 us
  local copies, waits for them, and re-layouts: 37.6 us -> 153 us
  blocking collectives: 102 us -> 0 us
  other arithmetic: 53.4 us -> 81.1 us
  between operations: 15.5 us -> 2.99 us
    reduce_scatter x9 -> x0, waiting for transfers between devices: 208 us -> none  [the longest x1 36.6 us: on_device(): lax.psum_scatter(gate_grad.astype(jnp.bfloat16), 'fsdp', scatter_dimensio...]
    psum x4 -> x0, waiting for transfers between devices: 177 us -> none  [the longest x1 69.7 us: on_device(): lax.psum(jnp.dot(activated, d_full, preferred_element_type=jnp.float32).a...]
    ppermute x0 -> x80, starting transfers between devices: none -> 129 us  [the longest x78 123 us: flip(): return lax.ppermute(values, axis_name, [(i, i ^ bit) for i in range(size)])]
    ppermute x0 -> x80, waiting for transfers between devices: none -> 111 us  [the longest x78 111 us: flip(): return lax.ppermute(values, axis_name, [(i, i ^ bit) for i in range(size)])]
    all_gather x5 -> x0, waiting for transfers between devices: 101 us -> none  [the longest x1 34.7 us: on_device(): lax.all_gather(w_up, 'fsdp', axis=0, tiled=True)]
    all_gather x4 -> x0, blocking collectives: 62.3 us -> none  [the longest x1 24 us: on_device(): lax.all_gather(key_projection, 'fsdp', axis=0, tiled=True)]
    unnamed x117 -> x258, local copies, waits for them, and re-layouts: 11.1 us -> 63.7 us
    psum x1 -> x0, blocking collectives: 39.9 us -> none  [on_device(): lax.psum((attn_gain_part * share, q_gain_part, k_gain_part, ffn_gain_part...]
  transfers between devices with their start and end apart: 18 -> 80, of which waited for: 15 -> 24; matrix products, arithmetic and copies ran while one was open for 15% -> 52% of each run, Pallas kernels for 0% -> 0%
where the time goes in v1:
time: 576 us; the launch traced here: 567 us
  local copies, waits for them, and re-layouts  153 us (27%)
  starting transfers between devices  129 us (22%)
  waiting for transfers between devices  111 us (19%)
  matrix products  89.5 us (16%)
  other arithmetic  81.1 us (14%)
    ppermute x78, starting transfers between devices, flip(): return lax.ppermute(values, axis_name, [(i, i ^ bit) for i in range(size)])  123 us
    ppermute x78, waiting for transfers between devices, flip(): return lax.ppermute(values, axis_name, [(i, i ^ bit) for i in range(size)])  111 us
    unnamed x258, local copies, waits for them, and re-layouts  63.7 us
    dot_general x4, matrix products, permute(): out = jnp.einsum(spec, high, order, preferred_element_type=jnp.float32)  19.3 us
    dynamic_slice x8, local copies, waits for them, and re-layouts, tensor_sum(): sent = lax.dynamic_index_in_dim(pieces[chunk], 1 - core, 0, keepdims=False)  16 us
  transfers between devices with their start and end apart: 80, of which 24 were waited for; matrix products, arithmetic and copies ran while one was open for 52% of the time, Pallas kernels for 0%

profile of v1, /device:TPU:0, one launch (start us, length us, event | category | flops | bytes accessed | tf_op | source)
XLA Modules:
  0.0 567.2 jit_solution(8408883236648578119)
XLA Ops:
  4.6 5.0 collective-permute-start.2
  21.0 4.4 fusion.87
  41.0 8.4 %collective-permute-done.3 = bf16[128,1024]{1,0:T(8,128)(2,1)S(1)} collective-permute-done((bf16[128,1024]{1,0:T(8,128)(2,1)}, bf16[128,1024]{1,0:T(8,128)(2,1)S(1)}, u32[]{:S(2)}, u32[]{:S(2)}) %collective-permute-start.3) | collective-permute-done | bytes 262176 | tf_op jit(solution)/shard_map/ppermute | solution.py:54
  52.4 3.5 collective-permute-start.9
  57.6 3.5 collective-permute-start.27
  61.2 3.5 fusion.187
  101.4 5.2 fusion.110
  115.2 3.5 collective-permute-start.21
  142.6 4.4 collective-permute-start.6
  154.7 14.6 %collective-permute-done.30 = bf16[768,128]{1,0:T(8,128)(2,1)S(1)} collective-permute-done((bf16[768,128]{1,0:T(8,128)(2,1)}, bf16[768,128]{1,0:T(8,128)(2,1)S(1)}, u32[]{:S(2)}, u32[]{:S(2)}) %collective-permute-start.30) | collective-permute-done | bytes 196640 | tf_op jit(solution)/shard_map/ppermute | solution.py:54
  204.1 10.8 %collective-permute-done.17 = bf16[192,1024]{0,1:T(8,128)(2,1)S(1)} collective-permute-done((bf16[192,1024]{0,1:T(8,128)(2,1)S(1)}, bf16[192,1024]{0,1:T(8,128)(2,1)S(1)}, u32[]{:S(2)}, u32[]{:S(2)}) %collective-permute-start.17) | collective-permute-done | bytes 393248 | tf_op jit(solution)/shard_map/ppermute | solution.py:54
  215.1 10.1 %collective-permute-done.14 = bf16[192,1024]{0,1:T(8,128)(2,1)S(1)} collective-permute-done((bf16[192,1024]{0,1:T(8,128)(2,1)S(1)}, bf16[192,1024]{0,1:T(8,128)(2,1)S(1)}, u32[]{:S(2)}, u32[]{:S(2)}) %collective-permute-start.14) | collective-permute-done | bytes 393248 | tf_op jit(solution)/shard_map/ppermute | solution.py:54
  234.8 4.3 fusion.202
  239.1 4.7 convolution_convert_fusion
  246.3 18.6 %collective-permute-start.75 = (bf16[768,512]{1,0:T(8,128)(2,1)}, bf16[768,512]{1,0:T(8,128)(2,1)}, u32[]{:S(2)}, u32[]{:S(2)}) collective-permute-start(bf16[768,512]{1,0:T(8,128)(2,1)} %slice.422), channel_id=1, source_target_pairs={{0,4},{4,0},{1,5},{5,1},{2,6},{6,2},{3,7},{7,3},{8,12},{12,8},{9,1... | collective-permute-start | bytes 2359304 | tf_op jit(solution)/shard_map/ppermute | solution.py:54
  273.4 4.3 convolution_convert_fusion.3
  284.3 3.5 copy.370
  298.1 6.0 %collective-permute-done.35 = bf16[192,1024]{0,1:T(8,128)(2,1)S(1)} collective-permute-done((bf16[192,1024]{0,1:T(8,128)(2,1)S(1)}, bf16[192,1024]{0,1:T(8,128)(2,1)S(1)}, u32[]{:S(2)}, u32[]{:S(2)}) %collective-permute-start.35) | collective-permute-done | bytes 393248 | tf_op jit(solution)/shard_map/ppermute | solution.py:54
  306.4 8.3 %collective-permute-done.32 = bf16[192,1024]{0,1:T(8,128)(2,1)S(1)} collective-permute-done((bf16[192,1024]{0,1:T(8,128)(2,1)S(1)}, bf16[192,1024]{0,1:T(8,128)(2,1)S(1)}, u32[]{:S(2)}, u32[]{:S(2)}) %collective-permute-start.32) | collective-permute-done | bytes 393248 | tf_op jit(solution)/shard_map/ppermute | solution.py:54
  319.4 3.6 multiply_reduce_fusion
  329.7 6.1 %multiply_convert_fusion.1 = bf16[2,2,768,768]{2,3,1,0:T(8,128)(2,1)} fusion(f32[2,768,768,2]{2,1,3,0:T(8,128)S(1)} %bitcast.377, f32[2,2,768]{2,1,0:T(2,128)} %get-tuple-element.329, f32[2,2,768]{2,1,0:T(2,128)} %log_add_fusion, pred[768,768]{0,1:T(8,128)(4,1)S(1)} %copy-done.16, bf16[2,2,768,128]{2,3,1,0:T(8,128)(2,1)} %bitcast.46, ...), kind=kOutput, calls=%fused_computation.49 | convolution fusion | flops 618135552 | bytes 15949824 | tf_op jit(solution)/shard_map/kgqd,skd->kgqs/dot_general | solution.py:346
  354.5 4.0 bitcast_add_fusion.2
  382.0 16.5 %collective-permute-start.55 = (bf16[512,512]{1,0:T(8,128)(2,1)S(1)}, bf16[512,512]{1,0:T(8,128)(2,1)S(1)}, u32[]{:S(2)}, u32[]{:S(2)}) collective-permute-start(bf16[512,512]{1,0:T(8,128)(2,1)S(1)} %slice.381), channel_id=1, source_target_pairs={{0,4},{4,0},{1,5},{5,1},{2,6},{6,2},{3,7},{7,3},{8,12},{12,8},{9,1... | collective-permute-start | bytes 1572872 | tf_op jit(solution)/shard_map/ppermute | solution.py:54
  408.6 3.6 collective-permute-start.68
  412.1 11.0 %collective-permute-done.55 = bf16[512,512]{1,0:T(8,128)(2,1)S(1)} collective-permute-done((bf16[512,512]{1,0:T(8,128)(2,1)S(1)}, bf16[512,512]{1,0:T(8,128)(2,1)S(1)}, u32[]{:S(2)}, u32[]{:S(2)}) %collective-permute-start.55) | collective-permute-done | bytes 524320 | tf_op jit(solution)/shard_map/ppermute | solution.py:54
  427.7 7.9 %collective-permute-done.67 = bf16[512,128]{1,0:T(8,128)(2,1)S(1)} collective-permute-done((bf16[512,128]{1,0:T(8,128)(2,1)S(1)}, bf16[512,128]{1,0:T(8,128)(2,1)S(1)}, u32[]{:S(2)}, u32[]{:S(2)}) %collective-permute-start.67) | collective-permute-done | bytes 131104 | tf_op jit(solution)/shard_map/ppermute | solution.py:54
  437.5 13.1 %collective-permute-start.72 = (bf16[128,1536]{1,0:T(8,128)(2,1)}, bf16[128,1536]{1,0:T(8,128)(2,1)}, u32[]{:S(2)}, u32[]{:S(2)}) collective-permute-start(bf16[128,1536]{1,0:T(8,128)(2,1)} %get-tuple-element.221), channel_id=1, source_target_pairs={{0,16},{8,24},{16,0},{24,8},{1,17},{9,25},{17,1},{25,9},{2,18},{10... | collective-permute-start | bytes 1179656 | tf_op jit(solution)/shard_map/ppermute | solution.py:54
  450.5 10.4 %collective-permute-done.57 = bf16[128,512]{1,0:T(8,128)(2,1)S(1)} collective-permute-done((bf16[128,512]{1,0:T(8,128)(2,1)S(1)}, bf16[128,512]{1,0:T(8,128)(2,1)S(1)}, u32[]{:S(2)}, u32[]{:S(2)}) %collective-permute-start.57) | collective-permute-done | bytes 131104 | tf_op jit(solution)/shard_map/ppermute | solution.py:54
  479.8 3.5 fusion.203
  500.5 3.6 copy.369
  518.2 8.2 %fusion.90 = bf16[768,1024]{1,0:T(8,128)(2,1)} fusion(s32[1024]{0:T(1024)S(1)} %copy-done.95, bf16[1024,768]{1,0:T(8,128)(2,1)S(1)} %get-tuple-element.324, bf16[192,1024]{0,1:T(8,128)(2,1)S(1)} %get-tuple-element.268, bf16[192,1024]{0,1:T(8,128)(2,1)S(1)} %get-tuple-element.267, bf16[192,1024]{0,1:T(8,128)(2,1)S(1)} %get-tuple-element.266, ...), kind=kOutput, calls=%fused_computation.115 | convolution fusion | flops 1628176384 | bytes 6295552 | tf_op jit(solution)/shard_map/tc,rc->tr/dot_general | solution.py:85
  560.8 4.8 fusion.83
  (578 shorter events, 344.1 us)
Async XLA Ops:
  4.6 26.0 %collective-permute-start.2 = (bf16[128,1024]{1,0:T(8,128)(2,1)}, bf16[128,1024]{1,0:T(8,128)(2,1)}, u32[]{:S(2)}, u32[]{:S(2)}) collective-permute-start(bf16[128,1024]{1,0:T(8,128)(2,1)} %get-tuple-element.212), channel_id=1, source_target_pairs={{0,24},{8,16},{16,8},{24,0},{1,25},{9,17},{17,9},{25,1},{2,26},{10... | collective-permute-start | bytes 786440 | tf_op jit(solution)/shard_map/ppermute | solution.py:54
  9.6 22.6 %collective-permute-start.1 = (bf16[128,1024]{1,0:T(8,128)(2,1)}, bf16[128,1024]{1,0:T(8,128)(2,1)}, u32[]{:S(2)}, u32[]{:S(2)}) collective-permute-start(bf16[128,1024]{1,0:T(8,128)(2,1)} %get-tuple-element.212), channel_id=1, source_target_pairs={{0,16},{8,24},{16,0},{24,8},{1,17},{9,25},{17,1},{25,9},{2,18},{10... | collective-permute-start | bytes 786440 | tf_op jit(solution)/shard_map/ppermute | solution.py:54
  9.6 24.1 %collective-permute-start = (bf16[128,1024]{1,0:T(8,128)(2,1)}, bf16[128,1024]{1,0:T(8,128)(2,1)}, u32[]{:S(2)}, u32[]{:S(2)}) collective-permute-start(bf16[128,1024]{1,0:T(8,128)(2,1)} %get-tuple-element.212), channel_id=1, source_target_pairs={{0,8},{8,0},{16,24},{24,16},{1,9},{9,1},{17,25},{25,17},{2,10},{10... | collective-permute-start | bytes 786440 | tf_op jit(solution)/shard_map/ppermute | solution.py:54
  52.4 67.8 %collective-permute-start.9 = (bf16[512,128]{1,0:T(8,128)(2,1)}, bf16[512,128]{1,0:T(8,128)(2,1)}, u32[]{:S(2)}, u32[]{:S(2)}) collective-permute-start(bf16[512,128]{1,0:T(8,128)(2,1)} %get-tuple-element.208), channel_id=1, source_target_pairs={{0,24},{8,16},{16,8},{24,0},{1,25},{9,17},{17,9},{25,1},{2,26},{10... | collective-permute-start | bytes 393224 | tf_op jit(solution)/shard_map/ppermute | solution.py:54
  56.0 59.2 %collective-permute-start.8 = (bf16[512,128]{1,0:T(8,128)(2,1)}, bf16[512,128]{1,0:T(8,128)(2,1)}, u32[]{:S(2)}, u32[]{:S(2)}) collective-permute-start(bf16[512,128]{1,0:T(8,128)(2,1)} %get-tuple-element.208), channel_id=1, source_target_pairs={{0,16},{8,24},{16,0},{24,8},{1,17},{9,25},{17,1},{25,9},{2,18},{10... | collective-permute-start | bytes 393224 | tf_op jit(solution)/shard_map/ppermute | solution.py:54
  56.0 56.7 %collective-permute-start.7 = (bf16[512,128]{1,0:T(8,128)(2,1)}, bf16[512,128]{1,0:T(8,128)(2,1)}, u32[]{:S(2)}, u32[]{:S(2)}) collective-permute-start(bf16[512,128]{1,0:T(8,128)(2,1)} %get-tuple-element.208), channel_id=1, source_target_pairs={{0,8},{8,0},{16,24},{24,16},{1,9},{9,1},{17,25},{25,17},{2,10},{10... | collective-permute-start | bytes 393224 | tf_op jit(solution)/shard_map/ppermute | solution.py:54
  57.6 70.6 %collective-permute-start.27 = (bf16[768,128]{1,0:T(8,128)(2,1)}, bf16[768,128]{1,0:T(8,128)(2,1)}, u32[]{:S(2)}, u32[]{:S(2)}) collective-permute-start(bf16[768,128]{1,0:T(8,128)(2,1)} %get-tuple-element.206), channel_id=1, source_target_pairs={{0,24},{8,16},{16,8},{24,0},{1,25},{9,17},{17,9},{25,1},{2,26},{10... | collective-permute-start | bytes 589832 | tf_op jit(solution)/shard_map/ppermute | solution.py:54
  61.2 64.0 %collective-permute-start.26 = (bf16[768,128]{1,0:T(8,128)(2,1)}, bf16[768,128]{1,0:T(8,128)(2,1)}, u32[]{:S(2)}, u32[]{:S(2)}) collective-permute-start(bf16[768,128]{1,0:T(8,128)(2,1)} %get-tuple-element.206), channel_id=1, source_target_pairs={{0,16},{8,24},{16,0},{24,8},{1,17},{9,25},{17,1},{25,9},{2,18},{10... | collective-permute-start | bytes 589832 | tf_op jit(solution)/shard_map/ppermute | solution.py:54
  115.2 34.1 %collective-permute-start.21 = (bf16[128,1536]{1,0:T(8,128)(2,1)}, bf16[128,1536]{1,0:T(8,128)(2,1)}, u32[]{:S(2)}, u32[]{:S(2)}) collective-permute-start(bf16[128,1536]{1,0:T(8,128)(2,1)} %get-tuple-element.210), channel_id=1, source_target_pairs={{0,24},{8,16},{16,8},{24,0},{1,25},{9,17},{17,9},{25,1},{2,26},{10... | collective-permute-start | bytes 1179656 | tf_op jit(solution)/shard_map/ppermute | solution.py:54
  120.3 29.9 %collective-permute-start.20 = (bf16[128,1536]{1,0:T(8,128)(2,1)}, bf16[128,1536]{1,0:T(8,128)(2,1)}, u32[]{:S(2)}, u32[]{:S(2)}) collective-permute-start(bf16[128,1536]{1,0:T(8,128)(2,1)} %get-tuple-element.210), channel_id=1, source_target_pairs={{0,16},{8,24},{16,0},{24,8},{1,17},{9,25},{17,1},{25,9},{2,18},{10... | collective-permute-start | bytes 1179656 | tf_op jit(solution)/shard_map/ppermute | solution.py:54
  123.5 27.8 %collective-permute-start.19 = (bf16[128,1536]{1,0:T(8,128)(2,1)}, bf16[128,1536]{1,0:T(8,128)(2,1)}, u32[]{:S(2)}, u32[]{:S(2)}) collective-permute-start(bf16[128,1536]{1,0:T(8,128)(2,1)} %get-tuple-element.210), channel_id=1, source_target_pairs={{0,8},{8,0},{16,24},{24,16},{1,9},{9,1},{17,25},{25,17},{2,10},{10... | collective-permute-start | bytes 1179656 | tf_op jit(solution)/shard_map/ppermute | solution.py:54
  142.6 31.7 %collective-permute-start.6 = (bf16[768,4,128]{2,0,1:T(8,128)(2,1)S(1)}, bf16[768,4,128]{2,0,1:T(8,128)(2,1)S(1)}, u32[]{:S(2)}, u32[]{:S(2)}) collective-permute-start(bf16[768,4,128]{2,0,1:T(8,128)(2,1)S(1)} %copy-done.62), channel_id=1, source_target_pairs={{0,4},{1,5},{2,6},{3,7},{8,12},{9,13},{10,14},{11,15},{16,20},{17,... | collective-permute-start | bytes 2359304 | tf_op jit(solution)/shard_map/ppermute | solution.py:263
  149.3 53.0 %collective-permute-start.24 = (bf16[128,1536]{1,0:T(8,128)(2,1)}, bf16[128,1536]{1,0:T(8,128)(2,1)}, u32[]{:S(2)}, u32[]{:S(2)}) collective-permute-start(bf16[128,1536]{1,0:T(8,128)(2,1)} %collective-permute-done.21), channel_id=1, source_target_pairs={{0,4},{4,0},{1,5},{5,1},{2,6},{6,2},{3,7},{7,3},{8,12},{12,8},{9,1... | collective-permute-start | bytes 1179656 | tf_op jit(solution)/shard_map/ppermute | solution.py:54
  150.1 46.9 %collective-permute-start.23 = (bf16[128,1536]{1,0:T(8,128)(2,1)}, bf16[128,1536]{1,0:T(8,128)(2,1)}, u32[]{:S(2)}, u32[]{:S(2)}) collective-permute-start(bf16[128,1536]{1,0:T(8,128)(2,1)} %collective-permute-done.20), channel_id=1, source_target_pairs={{0,4},{4,0},{1,5},{5,1},{2,6},{6,2},{3,7},{7,3},{8,12},{12,8},{9,1... | collective-permute-start | bytes 1179656 | tf_op jit(solution)/shard_map/ppermute | solution.py:54
  151.3 44.0 %collective-permute-start.22 = (bf16[128,1536]{1,0:T(8,128)(2,1)}, bf16[128,1536]{1,0:T(8,128)(2,1)}, u32[]{:S(2)}, u32[]{:S(2)}) collective-permute-start(bf16[128,1536]{1,0:T(8,128)(2,1)} %collective-permute-done.19), channel_id=1, source_target_pairs={{0,4},{4,0},{1,5},{5,1},{2,6},{6,2},{3,7},{7,3},{8,12},{12,8},{9,1... | collective-permute-start | bytes 1179656 | tf_op jit(solution)/shard_map/ppermute | solution.py:54
  201.7 23.4 %collective-permute-start.14 = (bf16[192,1024]{0,1:T(8,128)(2,1)S(1)}, bf16[192,1024]{0,1:T(8,128)(2,1)S(1)}, u32[]{:S(2)}, u32[]{:S(2)}) collective-permute-start(bf16[192,1024]{0,1:T(8,128)(2,1)S(1)} %fusion.125), channel_id=1, source_target_pairs={{0,2},{1,3},{2,0},{3,1},{4,6},{5,7},{6,4},{7,5},{8,10},{9,11},{10,... | collective-permute-start | bytes 1179656 | tf_op jit(solution)/shard_map/ppermute | solution.py:54
  246.3 46.5 %collective-permute-start.75 = (bf16[768,512]{1,0:T(8,128)(2,1)}, bf16[768,512]{1,0:T(8,128)(2,1)}, u32[]{:S(2)}, u32[]{:S(2)}) collective-permute-start(bf16[768,512]{1,0:T(8,128)(2,1)} %slice.422), channel_id=1, source_target_pairs={{0,4},{4,0},{1,5},{5,1},{2,6},{6,2},{3,7},{7,3},{8,12},{12,8},{9,1... | collective-permute-start | bytes 2359304 | tf_op jit(solution)/shard_map/ppermute | solution.py:54
  284.3 97.6 %collective-permute-start.70 = (bf16[512,1536]{1,0:T(8,128)(2,1)}, bf16[512,1536]{1,0:T(8,128)(2,1)}, u32[]{:S(2)}, u32[]{:S(2)}) collective-permute-start(bf16[512,1536]{1,0:T(8,128)(2,1)} %slice.411), channel_id=1, source_target_pairs={{0,4},{4,0},{1,5},{5,1},{2,6},{6,2},{3,7},{7,3},{8,12},{12,8},{9,1... | collective-permute-start | bytes 4718600 | tf_op jit(solution)/shard_map/ppermute | solution.py:54
  317.4 59.0 %collective-permute-start.79 = (bf16[768,128]{1,0:T(8,128)(2,1)}, bf16[768,128]{1,0:T(8,128)(2,1)}, u32[]{:S(2)}, u32[]{:S(2)}) collective-permute-start(bf16[768,128]{1,0:T(8,128)(2,1)} %add_convert_fusion.16), channel_id=1, source_target_pairs={{0,4},{4,0},{1,5},{5,1},{2,6},{6,2},{3,7},{7,3},{8,12},{12,8},{9,1... | collective-permute-start | bytes 589832 | tf_op jit(solution)/shard_map/ppermute | solution.py:54
  336.7 69.5 %collective-permute-start.65 = (bf16[512,512]{1,0:T(8,128)(2,1)}, bf16[512,512]{1,0:T(8,128)(2,1)}, u32[]{:S(2)}, u32[]{:S(2)}) collective-permute-start(bf16[512,512]{1,0:T(8,128)(2,1)} %slice.401), channel_id=1, source_target_pairs={{0,4},{4,0},{1,5},{5,1},{2,6},{6,2},{3,7},{7,3},{8,12},{12,8},{9,1... | collective-permute-start | bytes 1572872 | tf_op jit(solution)/shard_map/ppermute | solution.py:54
  351.0 50.2 %collective-permute-start.37 = (bf16[192,1024]{0,1:T(8,128)(2,1)}, bf16[192,1024]{0,1:T(8,128)(2,1)}, u32[]{:S(2)}, u32[]{:S(2)}) collective-permute-start(bf16[192,1024]{0,1:T(8,128)(2,1)} %bitcast.403), channel_id=1, source_target_pairs={{0,1},{1,0},{2,3},{3,2},{4,5},{5,4},{6,7},{7,6},{8,9},{9,8},{10,11... | collective-permute-start | bytes 1179656 | tf_op jit(solution)/shard_map/ppermute | solution.py:54
  351.0 53.1 %collective-permute-start.40 = (bf16[192,1024]{0,1:T(8,128)(2,1)}, bf16[192,1024]{0,1:T(8,128)(2,1)}, u32[]{:S(2)}, u32[]{:S(2)}) collective-permute-start(bf16[192,1024]{0,1:T(8,128)(2,1)} %bitcast.402), channel_id=1, source_target_pairs={{0,1},{1,0},{2,3},{3,2},{4,5},{5,4},{6,7},{7,6},{8,9},{9,8},{10,11... | collective-permute-start | bytes 1179656 | tf_op jit(solution)/shard_map/ppermute | solution.py:54
  376.4 86.7 %collective-permute-start.43 = (bf16[768,4,128]{2,0,1:T(8,128)(2,1)S(1)}, bf16[768,4,128]{2,0,1:T(8,128)(2,1)S(1)}, u32[]{:S(2)}, u32[]{:S(2)}) collective-permute-start(bf16[768,4,128]{2,0,1:T(8,128)(2,1)S(1)} %pad_maximum_fusion.9), channel_id=1, source_target_pairs={{4,0},{5,1},{6,2},{7,3},{12,8},{13,9},{14,10},{15,11},{20,16},{21,... | collective-permute-start | bytes 2359304 | tf_op jit(solution)/shard_map/ppermute | solution.py:381
  382.0 41.2 %collective-permute-start.55 = (bf16[512,512]{1,0:T(8,128)(2,1)S(1)}, bf16[512,512]{1,0:T(8,128)(2,1)S(1)}, u32[]{:S(2)}, u32[]{:S(2)}) collective-permute-start(bf16[512,512]{1,0:T(8,128)(2,1)S(1)} %slice.381), channel_id=1, source_target_pairs={{0,4},{4,0},{1,5},{5,1},{2,6},{6,2},{3,7},{7,3},{8,12},{12,8},{9,1... | collective-permute-start | bytes 1572872 | tf_op jit(solution)/shard_map/ppermute | solution.py:54
  401.2 82.1 %collective-permute-start.71 = (bf16[128,1536]{1,0:T(8,128)(2,1)}, bf16[128,1536]{1,0:T(8,128)(2,1)}, u32[]{:S(2)}, u32[]{:S(2)}) collective-permute-start(bf16[128,1536]{1,0:T(8,128)(2,1)} %get-tuple-element.219), channel_id=1, source_target_pairs={{0,8},{8,0},{16,24},{24,16},{1,9},{9,1},{17,25},{25,17},{2,10},{10... | collective-permute-start | bytes 1179656 | tf_op jit(solution)/shard_map/ppermute | solution.py:54
  435.6 25.3 %collective-permute-start.57 = (bf16[128,512]{1,0:T(8,128)(2,1)S(1)}, bf16[128,512]{1,0:T(8,128)(2,1)S(1)}, u32[]{:S(2)}, u32[]{:S(2)}) collective-permute-start(bf16[128,512]{1,0:T(8,128)(2,1)S(1)} %get-tuple-element.244), channel_id=1, source_target_pairs={{0,16},{8,24},{16,0},{24,8},{1,17},{9,25},{17,1},{25,9},{2,18},{10... | collective-permute-start | bytes 393224 | tf_op jit(solution)/shard_map/ppermute | solution.py:54
  437.3 46.0 %collective-permute-start.73 = (bf16[128,1536]{1,0:T(8,128)(2,1)}, bf16[128,1536]{1,0:T(8,128)(2,1)}, u32[]{:S(2)}, u32[]{:S(2)}) collective-permute-start(bf16[128,1536]{1,0:T(8,128)(2,1)} %get-tuple-element.220), channel_id=1, source_target_pairs={{0,24},{8,16},{16,8},{24,0},{1,25},{9,17},{17,9},{25,1},{2,26},{10... | collective-permute-start | bytes 1179656 | tf_op jit(solution)/shard_map/ppermute | solution.py:54
  437.5 47.8 %collective-permute-start.72 = (bf16[128,1536]{1,0:T(8,128)(2,1)}, bf16[128,1536]{1,0:T(8,128)(2,1)}, u32[]{:S(2)}, u32[]{:S(2)}) collective-permute-start(bf16[128,1536]{1,0:T(8,128)(2,1)} %get-tuple-element.221), channel_id=1, source_target_pairs={{0,16},{8,24},{16,0},{24,8},{1,17},{9,25},{17,1},{25,9},{2,18},{10... | collective-permute-start | bytes 1179656 | tf_op jit(solution)/shard_map/ppermute | solution.py:54
  460.9 44.1 %collective-permute-start.38 = (bf16[192,1024]{0,1:T(8,128)(2,1)}, bf16[192,1024]{0,1:T(8,128)(2,1)}, u32[]{:S(2)}, u32[]{:S(2)}) collective-permute-start(bf16[192,1024]{0,1:T(8,128)(2,1)} %fusion.121), channel_id=1, source_target_pairs={{0,2},{1,3},{2,0},{3,1},{4,6},{5,7},{6,4},{7,5},{8,10},{9,11},{10,... | collective-permute-start | bytes 1179656 | tf_op jit(solution)/shard_map/ppermute | solution.py:54
  463.2 43.2 %collective-permute-start.41 = (bf16[192,1024]{0,1:T(8,128)(2,1)}, bf16[192,1024]{0,1:T(8,128)(2,1)}, u32[]{:S(2)}, u32[]{:S(2)}) collective-permute-start(bf16[192,1024]{0,1:T(8,128)(2,1)} %fusion.120), channel_id=1, source_target_pairs={{0,2},{1,3},{2,0},{3,1},{4,6},{5,7},{6,4},{7,5},{8,10},{9,11},{10,... | collective-permute-start | bytes 1179656 | tf_op jit(solution)/shard_map/ppermute | solution.py:54
  483.3 49.2 %collective-permute-start.59 = (bf16[128,512]{1,0:T(8,128)(2,1)}, bf16[128,512]{1,0:T(8,128)(2,1)}, u32[]{:S(2)}, u32[]{:S(2)}) collective-permute-start(bf16[128,512]{1,0:T(8,128)(2,1)} %add_convert_fusion.28), channel_id=1, source_target_pairs={{0,4},{4,0},{1,5},{5,1},{2,6},{6,2},{3,7},{7,3},{8,12},{12,8},{9,1... | collective-permute-start | bytes 393224 | tf_op jit(solution)/shard_map/ppermute | solution.py:54
  489.7 23.7 %collective-permute-start.60 = (bf16[512,512]{1,0:T(8,128)(2,1)}, bf16[512,512]{1,0:T(8,128)(2,1)}, u32[]{:S(2)}, u32[]{:S(2)}) collective-permute-start(bf16[512,512]{1,0:T(8,128)(2,1)} %slice.390), channel_id=1, source_target_pairs={{0,4},{4,0},{1,5},{5,1},{2,6},{6,2},{3,7},{7,3},{8,12},{12,8},{9,1... | collective-permute-start | bytes 1572872 | tf_op jit(solution)/shard_map/ppermute | solution.py:54
  (156 other events, 1669.0 us)
